TPU v7x, 32 devices: a whole 2x2x4 slice. The times are simulated.
32 devices in a mesh: rep: 2 (over y), exp: 16 (over z, x, core).
Axes of the slice: x: 2, y: 2, z: 4, core: 2. Of those that a mesh axis runs over, the one named last changes fastest.
Arguments:
- cache_keys: bfloat16 [32, 2048, 512], P(('rep', 'exp')), may hold values from -6.5 to 6.5
- cache_values: bfloat16 [32, 2048, 512], P(('rep', 'exp')), may hold values from -6 to 6
- lengths: int32 [32], P(('rep', 'exp')), may hold values from 512 to 2048, as said below
- drift_rows: int32 [2, 32, 8], P(None, ('rep', 'exp')), may hold values from 0 to 2047, as said below
- block_in: bfloat16 [32, 8, 4096], P(('rep', 'exp')), may hold values from -6 to 6
- drift_in: bfloat16 [2, 32, 8, 4096], P(None, ('rep', 'exp')), may hold values from -6 to 6
- queries: bfloat16 [2, 32, 16, 4096], P(None, ('rep', 'exp')), may hold values from -150 to 150
- new_keys: bfloat16 [2, 32, 16, 512], P(None, ('rep', 'exp')), may hold values from -6 to 6
- new_values: bfloat16 [2, 32, 16, 512], P(None, ('rep', 'exp')), may hold values from -6 to 6
- norm_gain: float32 [4096], replicated, may hold values from 0.25 to 1.75
- expert_ids: int32 [2, 32, 16, 8], P(None, ('rep', 'exp')), may hold values from 0 to 15, all different within a row; in each aligned block of 16 rows (0 to 15, 16 to 31, ..., all dimensions but the last counted through in order) at most 12 rows name the same one
- gate_weights: bfloat16 [2, 32, 16, 8], P(None, ('rep', 'exp')), may hold values from 0.049804688 to 0.3984375
- w_gate: bfloat16 [16, 4096, 1024], P('exp', None, 'rep'), may hold values from -0.09375 to 0.09375
- w_up: bfloat16 [16, 4096, 1024], P('exp', None, 'rep'), may hold values from -0.09375 to 0.09375
- w_down: bfloat16 [16, 1024, 4096], P('exp', 'rep'), may hold values from -0.1875 to 0.1875
Outputs:
- out: bfloat16 [2, 32, 16, 4096], P(None, ('rep', 'exp'))
Inputs may be any that keep to these rules, and one draw needn't show every extreme that they name: `lengths`: one request has exactly 2048. `drift_rows`: for each step and request, 8 different positions in increasing order, all below that request's length. `expert_ids`: each row names 8 different experts; within one step the rows of one request name any expert at most 12 times, a bound that some block reaches.
All inputs are finite; a program needn't handle non-finite values.
Results may differ from a plain program's by a relative error of at most 0.012.
Values may be sent and summed in bfloat16 or wider, within the bound.
A program may use at most 128 MiB of HBM per device.

v0:
```python
import jax
import jax.numpy as jnp
from jax import lax
from jax.sharding import PartitionSpec as P

H = 32
KVH = 4
HD = 128
TOP = 8
BLOCK = 8


def attend(query_rows, key_rows, value_rows, block_keys, block_values, length):
    row_count = query_rows.shape[0]
    group_size = H // KVH
    query_head_rows = query_rows.reshape(row_count, KVH, group_size, HD)
    cache_k = key_rows.reshape(-1, KVH, HD)
    cached_value_rows = value_rows.reshape(-1, KVH, HD)
    prompt_key_rows = block_keys.reshape(-1, KVH, HD)
    prompt_value_rows = block_values.reshape(-1, KVH, HD)
    logit_scale_factor = HD ** (-0.5)
    cache_scores = (
        jnp.einsum("rkgd,ckd->kgrc", query_head_rows, cache_k, preferred_element_type=jnp.float32)
        * logit_scale_factor
    )
    prompt_score_rows = (
        jnp.einsum(
            "afhu,nfu->fhan", query_head_rows, prompt_key_rows, preferred_element_type=jnp.float32
        )
        * logit_scale_factor
    )
    cache_mask = jnp.arange(cache_k.shape[0]) < length
    own_mask = (jnp.arange(row_count) < BLOCK)[:, None]
    cache_scores = jnp.where(cache_mask, cache_scores, -1e30)
    prompt_score_rows = jnp.where(own_mask, prompt_score_rows, -1e30)
    peak = jnp.maximum(jnp.max(cache_scores, axis=-1), jnp.max(prompt_score_rows, axis=-1))
    cache_exp = jnp.exp(cache_scores - peak[..., None])
    own_exp = jnp.exp(prompt_score_rows - peak[..., None])
    denom = jnp.sum(cache_exp, axis=-1) + jnp.sum(own_exp, axis=-1)
    cached_weight_share = (cache_exp / denom[..., None]).astype(jnp.bfloat16)
    prompt_weight_share = (own_exp / denom[..., None]).astype(jnp.bfloat16)
    blended_output = jnp.einsum(
        "qimt,tqj->mqij", cached_weight_share, cached_value_rows, preferred_element_type=jnp.float32
    )
    blended_output = blended_output + jnp.einsum(
        "iywf,fie->wiye", prompt_weight_share, prompt_value_rows, preferred_element_type=jnp.float32
    )
    return blended_output.reshape(row_count, H * HD)


def route_table(routed, gate_share, experts, capacity):
    member = routed[:, :, None] == jnp.arange(experts)[None, None, :]
    weight = jnp.sum(jnp.where(member, gate_share[:, :, None].astype(jnp.float32), 0.0), axis=1)
    chosen = jnp.any(member, axis=1).astype(jnp.int32)
    slot_rank = jnp.cumsum(chosen, axis=0) - chosen
    taken = (slot_rank[:, :, None] == jnp.arange(capacity)[None, None, :]) & (
        chosen[:, :, None] == 1
    )
    return jnp.where(taken, weight[:, :, None], 0.0).astype(jnp.bfloat16)


def expert_terms(routed_rows, gate_part, up_part, down_part):
    flat_rows = routed_rows.reshape(-1, routed_rows.shape[-1])
    gate_act = jnp.dot(flat_rows, gate_part, preferred_element_type=jnp.float32)
    up_act = jnp.dot(flat_rows, up_part, preferred_element_type=jnp.float32)
    hidden = (jax.nn.silu(gate_act) * up_act).astype(jnp.bfloat16)
    produced = jnp.dot(hidden, down_part, preferred_element_type=jnp.float32).astype(jnp.bfloat16)
    return produced.reshape(routed_rows.shape)


def on_device(
    cache_keys,
    cache_values,
    lengths,
    drift_rows,
    block_in,
    drift_in,
    queries,
    new_keys,
    new_values,
    norm_gain,
    expert_ids,
    gate_weights,
    w_gate,
    w_up,
    w_down,
):
    rep_count = lax.axis_size("rep")
    experts = lax.axis_size("exp") * w_gate.shape[0]
    row_count = queries.shape[2]
    capacity = min(row_count, (3 * row_count * TOP + 2 * experts - 1) // (2 * experts))
    key_rows = cache_keys[0]
    value_rows = cache_values[0]
    carried = block_in[0]
    results = []
    for denoise in range(2):
        key_rows = key_rows.at[drift_rows[denoise, 0]].set(new_keys[denoise, 0, BLOCK:])
        value_rows = value_rows.at[drift_rows[denoise, 0]].set(new_values[denoise, 0, BLOCK:])
        attended = attend(
            queries[denoise, 0],
            key_rows,
            value_rows,
            new_keys[denoise, 0, :BLOCK],
            new_values[denoise, 0, :BLOCK],
            lengths[0],
        )
        inputs = jnp.concatenate([carried, drift_in[denoise, 0]], axis=0).astype(jnp.float32)
        residual = inputs + attended
        inverse = lax.rsqrt(jnp.mean(residual * residual, axis=-1, keepdims=True) + 1e-06)
        normed = (residual * inverse * norm_gain).astype(jnp.bfloat16)
        slot_table = route_table(
            expert_ids[denoise, 0], gate_weights[denoise, 0], experts, capacity
        )
        flat_table = slot_table.reshape(row_count, experts * capacity)
        all_rows, all_tables = (
            lax.all_gather(normed, "rep", axis=0, tiled=True),
            lax.all_gather(flat_table, "rep", axis=0, tiled=True),
        )
        all_rows = all_rows.reshape(rep_count, row_count, -1)
        all_tables = all_tables.reshape(rep_count, row_count, experts, capacity)
        chosen_slots = (all_tables != 0).astype(jnp.bfloat16)
        dispatched = jnp.einsum(
            "orec,ord->eocd", chosen_slots, all_rows, preferred_element_type=jnp.float32
        ).astype(jnp.bfloat16)
        produced = expert_terms(
            lax.all_to_all(dispatched, "exp", split_axis=0, concat_axis=0, tiled=True),
            w_gate[0],
            w_up[0],
            w_down[0],
        )
        expert_out = lax.all_to_all(produced, "exp", split_axis=0, concat_axis=0, tiled=True)
        combined = jnp.einsum(
            "orec,eocd->ord", all_tables, expert_out, preferred_element_type=jnp.float32
        )
        moe = lax.psum_scatter(
            combined.reshape(rep_count * row_count, -1).astype(jnp.bfloat16),
            "rep",
            scatter_dimension=0,
            tiled=True,
        ).astype(jnp.float32)
        result = (residual + moe).astype(jnp.bfloat16)
        results.append(result)
        carried = result[:BLOCK]
    return jnp.stack(results)[:, None]


def solution(mesh):
    placed = (
        P(("rep", "exp"), None, None),
        P(("rep", "exp"), None, None),
        P(("rep", "exp")),
        P(None, ("rep", "exp"), None),
        P(("rep", "exp"), None, None),
        P(None, ("rep", "exp"), None, None),
        P(None, ("rep", "exp"), None, None),
        P(None, ("rep", "exp"), None, None),
        P(None, ("rep", "exp"), None, None),
        P(),
        P(None, ("rep", "exp"), None, None),
        P(None, ("rep", "exp"), None, None),
        P("exp", None, "rep"),
        P("exp", None, "rep"),
        P("exp", "rep", None),
    )
    return jax.shard_map(
        on_device,
        mesh=mesh,
        in_specs=placed,
        out_specs=P(None, ("rep", "exp"), None, None),
        check_vma=False,
    )
```

profile of v0, /device:TPU:0, one launch (start us, length us, event | category | flops | bytes accessed | tf_op | source)
XLA Modules:
  0.0 490.8 jit_solution(2397583738535303850)
XLA Ops:
  6.6 0.6 copy-done.19
  9.6 5.3 %all_gather.12 = bf16[32,192]{1,0:T(8,128)(2,1)S(1)} all-gather(bf16[16,192]{1,0:T(8,128)(2,1)S(1)} %get-tuple-element.21), channel_id=1, replica_groups=mesh['rep'=2,'exp'=16] {'rep'}, dimensions={0}, use_global_device_ids=true | all-gather | bytes 18432 | tf_op jit(solution)/shard_map/all_gather | solution.py:117
  16.2 1.9 scatter_custom_fusion.1
  18.1 2.2 reshape.211
  20.4 4.1 scatter_custom_fusion.3
  24.5 4.0 reshape.218
  28.5 1.9 scatter_custom_fusion
  30.3 2.1 reshape.210
  32.4 0.4 fusion.109
  32.9 2.8 bitcast_reduce_fusion.1
  35.7 3.3 fusion.16
  39.1 1.3 fusion.42
  41.1 17.0 %all_gather.13 = bf16[32,4096]{1,0:T(8,128)(2,1)S(1)} all-gather(bf16[16,4096]{1,0:T(8,128)(2,1)S(1)} %multiply_convert_fusion.1), channel_id=1, replica_groups=mesh['rep'=2,'exp'=16] {'rep'}, dimensions={0}, use_global_device_ids=true | all-gather | bytes 393216 | tf_op jit(solution)/shard_map/all_gather | solution.py:116
  58.1 1.0 fusion
  59.0 3.3 copy.109
  62.3 76.0 %all_to_all.20 = bf16[16,2,12,4096]{3,1,2,0:T(2,128)(2,1)S(1)} all-to-all(bf16[16,2,12,4096]{3,1,2,0:T(2,128)(2,1)S(1)} %copy.109), channel_id=1, replica_groups=mesh['rep'=2,'exp'=16] {'exp'}, dimensions={0} | all-to-all | bytes 6291456 | tf_op jit(solution)/shard_map/all_to_all | solution.py:126
  138.3 4.4 copy.110
  142.8 5.6 %reshape.215 = bf16[384,4096]{1,0:T(8,128)(2,1)} reshape(bf16[16,2,12,4096]{3,2,1,0:T(8,128)(2,1)} %copy.110) | data formatting | bytes 6291456 | tf_op jit(solution)/shard_map/reshape | solution.py:63
  148.3 5.8 %fusion.13 = f32[384,512]{1,0:T(8,128)} fusion(bf16[384,4096]{1,0:T(8,128)(2,1)} %reshape.215, bf16[1,4096,512]{2,1,0:T(8,128)(2,1)} %param.27), kind=kOutput, calls=%fused_computation.25 | convolution fusion | flops 1610612736 | bytes 8126464 | tf_op jit(solution)/shard_map/dot_general | solution.py:64
  154.1 9.9 %convolution_convert_fusion.3 = bf16[384,4096]{1,0:T(8,128)(2,1)} fusion(bf16[1,512,4096]{2,1,0:T(8,128)(2,1)} %param.29, bf16[384,4096]{1,0:T(8,128)(2,1)} %reshape.215, bf16[1,4096,512]{2,1,0:T(8,128)(2,1)} %param.28, f32[384,512]{1,0:T(8,128)} %fusion.13), kind=kOutput, calls=%fused_computation.7 | convolution fusion | flops 3223977984 | bytes 15466496 | tf_op jit(solution)/shard_map/dot_general | solution.py:67
  164.0 5.5 %reshape.216 = bf16[16,2,12,4096]{3,2,1,0:T(8,128)(2,1)} reshape(bf16[384,4096]{1,0:T(8,128)(2,1)} %convolution_convert_fusion.3) | data formatting | bytes 6291456 | tf_op jit(solution)/shard_map/reshape | solution.py:68
  169.5 7.2 %copy.111 = bf16[16,2,12,4096]{3,1,2,0:T(2,128)(2,1)} copy(bf16[16,2,12,4096]{3,2,1,0:T(8,128)(2,1)} %reshape.216) | data formatting | bytes 6291456 | tf_op jit(solution)/shard_map/reshape | solution.py:68
  176.8 5.2 %all-to-all-start.1 = ((bf16[16,2,12,4096]{3,1,2,0:T(2,128)(2,1)}), bf16[16,2,12,4096]{3,1,2,0:T(2,128)(2,1)}, u32[]{:S(2)}, u32[]{:S(2)}) async-start(bf16[16,2,12,4096]{3,1,2,0:T(2,128)(2,1)} %copy.111), calls=%async_computation.1 | async-start | bytes 6291456 | tf_op jit(solution)/shard_map/all_to_all | solution.py:131
  182.1 1.9 scatter_custom_fusion.2
  184.0 4.8 all_gather.14
  189.2 2.1 reshape.217
  191.9 3.3 fusion.17
  195.1 46.3 %all-to-all-done.1 = bf16[16,2,12,4096]{3,1,2,0:T(2,128)(2,1)} async-done(((bf16[16,2,12,4096]{3,1,2,0:T(2,128)(2,1)}), bf16[16,2,12,4096]{3,1,2,0:T(2,128)(2,1)}, u32[]{:S(2)}, u32[]{:S(2)}) %all-to-all-start.1) | async-done | bytes 3145760 | tf_op jit(solution)/shard_map/all_to_all | solution.py:131
  241.4 6.0 %fusion.2 = bf16[2,16,4096]{2,1,0:T(8,128)(2,1)} fusion(bf16[2,16,16,12]{1,2,3,0:T(8,128)(2,1)S(1)} %copy.108, bf16[16,2,12,4096]{3,1,2,0:T(2,128)(2,1)} %all-to-all-done.1), kind=kOutput, calls=%fused_computation.12 | convolution fusion | flops 50462720 | bytes 3420160 | tf_op jit(solution)/shard_map/orec,eocd->ord/dot_general | solution.py:132
  247.5 4.2 fusion.45
  251.7 18.3 %reduce-scatter.3.cloned.1.call-done = bf16[16,4096]{1,0:T(8,128)(2,1)} async-done(((bf16[32,4096]{1,0:T(8,128)(2,1)}), bf16[16,4096]{1,0:T(8,128)(2,1)}) %reduce-scatter.3.cloned.1.call-update) | async-done | bytes 131088 | tf_op jit(solution)/shard_map/reduce_scatter | solution.py:135
  270.0 1.1 add_convert_fusion.1
  271.1 1.4 multiply_reduce_fusion
  272.8 5.9 %all_gather.15 = bf16[32,4096]{1,0:T(8,128)(2,1)S(1)} all-gather(bf16[16,4096]{1,0:T(8,128)(2,1)S(1)} %multiply_convert_fusion), channel_id=1, replica_groups=mesh['rep'=2,'exp'=16] {'rep'}, dimensions={0}, use_global_device_ids=true | all-gather | bytes 393216 | tf_op jit(solution)/shard_map/all_gather | solution.py:116
  278.7 0.9 fusion.1
  279.6 3.3 copy.122
  282.9 75.4 %all_to_all.21 = bf16[16,2,12,4096]{3,1,2,0:T(2,128)(2,1)S(1)} all-to-all(bf16[16,2,12,4096]{3,1,2,0:T(2,128)(2,1)S(1)} %copy.122), channel_id=1, replica_groups=mesh['rep'=2,'exp'=16] {'exp'}, dimensions={0} | all-to-all | bytes 6291456 | tf_op jit(solution)/shard_map/all_to_all | solution.py:126
  358.3 4.4 copy.123
  362.7 4.0 reshape.222
  366.7 4.8 fusion.11
  371.5 8.9 %convolution_convert_fusion.2 = bf16[384,4096]{1,0:T(8,128)(2,1)} fusion(bf16[1,512,4096]{2,1,0:T(8,128)(2,1)} %param.29, bf16[384,4096]{1,0:T(8,128)(2,1)S(1)} %reshape.222, bf16[1,4096,512]{2,1,0:T(8,128)(2,1)} %param.28, f32[384,512]{1,0:T(8,128)} %fusion.11), kind=kOutput, calls=%fused_computation.6 | convolution fusion | flops 3223977984 | bytes 15466496 | tf_op jit(solution)/shard_map/dot_general | solution.py:67
  380.5 5.5 %reshape.223 = bf16[16,2,12,4096]{3,2,1,0:T(8,128)(2,1)} reshape(bf16[384,4096]{1,0:T(8,128)(2,1)} %convolution_convert_fusion.2) | data formatting | bytes 6291456 | tf_op jit(solution)/shard_map/reshape | solution.py:68
  386.0 5.5 %copy.124 = bf16[16,2,12,4096]{3,1,2,0:T(2,128)(2,1)S(1)} copy(bf16[16,2,12,4096]{3,2,1,0:T(8,128)(2,1)} %reshape.223) | data formatting | bytes 6291456 | tf_op jit(solution)/shard_map/reshape | solution.py:68
  391.4 75.0 %all_to_all.22 = bf16[16,2,12,4096]{3,1,2,0:T(2,128)(2,1)S(1)} all-to-all(bf16[16,2,12,4096]{3,1,2,0:T(2,128)(2,1)S(1)} %copy.124), channel_id=1, replica_groups=mesh['rep'=2,'exp'=16] {'exp'}, dimensions={0} | all-to-all | bytes 6291456 | tf_op jit(solution)/shard_map/all_to_all | solution.py:131
  466.4 4.1 fusion.3
  470.5 11.4 %reduce-scatter.5.cloned.1.call-done = bf16[16,4096]{1,0:T(8,128)(2,1)} async-done(((bf16[32,4096]{1,0:T(8,128)(2,1)}), bf16[16,4096]{1,0:T(8,128)(2,1)}) %reduce-scatter.5.cloned.1.call-update) | async-done | bytes 131088 | tf_op jit(solution)/shard_map/reduce_scatter | solution.py:135
  481.9 1.1 fusion.62
  483.0 0.7 maximum_bitcast_fusion
  (102 shorter events, 5.0 us)
Async XLA Ops:
  6.5 0.7 copy-start.19
  6.5 0.8 copy-start.18
  6.5 3.0 copy-start.14
  6.5 9.5 %copy-start.13 = (bf16[2,1,16,4096]{3,2,1,0:T(8,128)(2,1)S(1)}, bf16[2,1,16,4096]{3,2,1,0:T(8,128)(2,1)}, u32[]{:S(2)}) copy-start(bf16[2,1,16,4096]{3,2,1,0:T(8,128)(2,1)} %param.21) | copy-start | bytes 786436
  6.5 9.6 %copy-start.20 = (s32[2,1,8]{2,1,0:T(1,128)S(1)}, s32[2,1,8]{2,1,0:T(1,128)}, u32[]{:S(2)}) copy-start(s32[2,1,8]{2,1,0:T(1,128)} %param.18) | copy-start | bytes 196
  6.5 9.6 %copy-start.2 = (bf16[1,2048,512]{2,1,0:T(8,128)(2,1)S(1)}, bf16[1,2048,512]{2,1,0:T(8,128)(2,1)}, u32[]{:S(2)}) copy-start(bf16[1,2048,512]{2,1,0:T(8,128)(2,1)} %param.15) | copy-start | bytes 6291460
  6.6 9.6 %copy-start.16 = (bf16[2,1,16,512]{3,2,1,0:T(8,128)(2,1)S(1)}, bf16[2,1,16,512]{3,2,1,0:T(8,128)(2,1)}, u32[]{:S(2)}) copy-start(bf16[2,1,16,512]{3,2,1,0:T(8,128)(2,1)} %param.22) | copy-start | bytes 98308
  9.6 263.0 %copy-start.10 = (bf16[8,4096]{1,0:T(8,128)(2,1)}, bf16[8,4096]{1,0:T(8,128)(2,1)S(1)}, u32[]{:S(2)}) copy-start(bf16[8,4096]{1,0:T(8,128)(2,1)S(1)} %get-tuple-element.9) | copy-start | bytes 196612
  18.1 2.3 copy-start.1
  20.3 8.1 %copy-start = (bf16[1,2048,512]{2,1,0:T(8,128)(2,1)S(1)}, bf16[1,2048,512]{2,1,0:T(8,128)(2,1)}, u32[]{:S(2)}) copy-start(bf16[1,2048,512]{2,1,0:T(8,128)(2,1)} %param.16) | copy-start | bytes 6291460
  20.3 8.1 %copy-start.17 = (bf16[2,1,16,512]{3,2,1,0:T(8,128)(2,1)S(1)}, bf16[2,1,16,512]{3,2,1,0:T(8,128)(2,1)}, u32[]{:S(2)}) copy-start(bf16[2,1,16,512]{3,2,1,0:T(8,128)(2,1)} %param.23) | copy-start | bytes 98308
  32.9 2.8 copy-start.4
  35.7 3.4 copy-start.5
  39.1 1.3 copy-start.12
  39.1 1.8 copy-start.15
  176.8 64.7 %all-to-all-start.1 = ((bf16[16,2,12,4096]{3,1,2,0:T(2,128)(2,1)}), bf16[16,2,12,4096]{3,1,2,0:T(2,128)(2,1)}, u32[]{:S(2)}, u32[]{:S(2)}) async-start(bf16[16,2,12,4096]{3,1,2,0:T(2,128)(2,1)} %copy.111), calls=%async_computation.1 | async-start | bytes 6291456 | tf_op jit(solution)/shard_map/all_to_all | solution.py:131
  182.0 88.0 %reduce-scatter.3.cloned.1.call-start = ((), (), s32[]{:S(2)}) async-start(), calls=%async_computation.6 | async-start | bytes 393216 | tf_op jit(solution)/shard_map/reduce_scatter | solution.py:135
  191.8 55.7 %copy-start.3 = (bf16[2048,4,128]{2,1,0:T(4,128)(2,1)S(1)}, bf16[2048,4,128]{2,1,0:T(4,128)(2,1)}, u32[]{:S(2)}) copy-start(bf16[2048,4,128]{2,1,0:T(4,128)(2,1)} %reshape.217) | copy-start | bytes 6291460
  247.4 234.5 %reduce-scatter.5.cloned.1.call-start = ((), (), s32[]{:S(2)}) async-start(), calls=%async_computation.7 | async-start | bytes 393216 | tf_op jit(solution)/shard_map/reduce_scatter | solution.py:135
  271.1 11.9 %copy-start.6 = (bf16[16,4096]{1,0:T(8,128)(2,1)}, bf16[16,4096]{1,0:T(8,128)(2,1)S(1)}, u32[]{:S(2)}) copy-start(bf16[16,4096]{1,0:T(8,128)(2,1)S(1)} %add_convert_fusion.1) | copy-start | bytes 393220
  271.1 11.8 %copy-start.8 = (bf16[8,4096]{1,0:T(8,128)(2,1)}, bf16[8,4096]{1,0:T(8,128)(2,1)S(1)}, u32[]{:S(2)}) copy-start(bf16[8,4096]{1,0:T(8,128)(2,1)S(1)} %slice.78) | copy-start | bytes 196612
  466.4 15.5 %copy-start.9 = (bf16[8,4096]{1,0:T(8,128)(2,1)S(1)}, bf16[8,4096]{1,0:T(8,128)(2,1)}, u32[]{:S(2)}) copy-start(bf16[8,4096]{1,0:T(8,128)(2,1)} %copy-done.8) | copy-start | bytes 196612
  466.4 15.5 %copy-start.11 = (bf16[8,4096]{1,0:T(8,128)(2,1)S(1)}, bf16[8,4096]{1,0:T(8,128)(2,1)}, u32[]{:S(2)}) copy-start(bf16[8,4096]{1,0:T(8,128)(2,1)} %copy-done.10) | copy-start | bytes 196612
  466.4 16.6 %copy-start.7 = (bf16[16,4096]{1,0:T(8,128)(2,1)S(1)}, bf16[16,4096]{1,0:T(8,128)(2,1)}, u32[]{:S(2)}) copy-start(bf16[16,4096]{1,0:T(8,128)(2,1)} %copy-done.6) | copy-start | bytes 393220
Sparse Core Ops, SparseCore 0:
  247.6 22.3 reduce-scatter.2
  470.6 11.2 reduce-scatter.4
where the time goes:
time: 493 us; the launch traced here: 491 us
  blocking collectives  259 us (53%)
  waiting for transfers between devices  76 us (15%)
  local copies, waits for them, and re-layouts  72.4 us (15%)
  matrix products  55.7 us (11%)
  between operations  14.9 us (3%)
  other arithmetic  7.2 us (1%)
  starting transfers between devices  5.31 us (1%)
    all_to_all x2, blocking collectives, on_device(): lax.all_to_all(dispatched, 'exp', split_axis=0, concat_axis=0, tiled=True)  151 us
    all_to_all x1, blocking collectives, on_device(): lax.all_to_all(produced, 'exp', split_axis=0, concat_axis=0, tiled=True)  75 us
    all_to_all x1, waiting for transfers between devices, on_device(): lax.all_to_all(produced, 'exp', split_axis=0, concat_axis=0, tiled=True)  46.3 us
    reduce_scatter x2, waiting for transfers between devices, on_device(): lax.psum_scatter(combined.reshape(rep_count * row_count, -1).astype(jnp.b...  29.7 us
    reshape x4, local copies, waits for them, and re-layouts, expert_terms(): return produced.reshape(routed_rows.shape)  23.7 us
    all_gather x2, blocking collectives, on_device(): lax.all_gather(normed, 'rep', axis=0, tiled=True)  22.9 us
    dot_general x2, matrix products, expert_terms(): jnp.dot(hidden, down_part, preferred_element_type=jnp.float32)  18.8 us
    dot_general x2, matrix products, expert_terms(): gate_act = jnp.dot(flat_rows, gate_part, preferred_element_type=jnp.float32)  10.7 us
  transfers between devices with their start and end apart: 3, of which 3 were waited for; matrix products, arithmetic and copies ran while one was open for 3% of the time, Pallas kernels for 0%

commit v1 on v0

--- a/solution.py
+++ b/solution.py
@@ -1,6 +1,8 @@
 import jax
 import jax.numpy as jnp
 from jax import lax
+from jax.experimental import pallas as pl
+from jax.experimental.pallas import tpu as pltpu
 from jax.sharding import PartitionSpec as P
 
 H = 32
@@ -144,7 +146,318 @@
     return jnp.stack(results)[:, None]
 
 
+GROUP = H // KVH
+EXTRA = 128
+
+
+def attention_kernel(q_ref, k_ref, v_ref, xk_ref, xv_ref, mask_ref, xmask_ref, out_ref):
+    scale = HD ** (-0.5)
+    keys, values = k_ref[...], v_ref[...]
+    row_count = q_ref.shape[1]
+    for step in range(2):
+        q = jnp.concatenate(
+            [q_ref[step, :, g * HD : (g + 1) * HD] for g in range(GROUP)], axis=0
+        )
+        nt = (((1,), (1,)), ((), ()))
+        scores = lax.dot_general(q, keys, nt, preferred_element_type=jnp.float32)
+        scores = scores * scale + mask_ref[step]
+        extra = lax.dot_general(q, xk_ref[step], nt, preferred_element_type=jnp.float32)
+        extra = extra * scale + xmask_ref[step]
+        peak = jnp.maximum(
+            jnp.max(scores, axis=1, keepdims=True), jnp.max(extra, axis=1, keepdims=True)
+        )
+        scores = jnp.exp(scores - peak)
+        extra = jnp.exp(extra - peak)
+        denom = jnp.sum(scores, axis=1, keepdims=True) + jnp.sum(extra, axis=1, keepdims=True)
+        mixed = jnp.dot(scores.astype(jnp.bfloat16), values, preferred_element_type=jnp.float32)
+        mixed += jnp.dot(
+            extra.astype(jnp.bfloat16), xv_ref[step], preferred_element_type=jnp.float32
+        )
+        mixed = mixed / denom
+        for g in range(GROUP):
+            out_ref[step, :, g * HD : (g + 1) * HD] = mixed[g * row_count : (g + 1) * row_count]
+
+
+def attend_both(keys, values, length, drift, queries, new_keys, new_values):
+    row_count, slots = queries.shape[1], keys.shape[0]
+    places = jnp.arange(slots)
+    hit = jnp.any(places[None, None, :] == drift[:, :, None], axis=1)
+    valid = places < length
+    open_ = jnp.stack([valid & ~hit[0], valid & ~hit[0] & ~hit[1]])
+    mask = jnp.where(open_, 0.0, -1e30).astype(jnp.float32)[:, None, :]
+    kept = ~jnp.any(drift[0][:, None] == drift[1][None, :], axis=1)
+    own = (jnp.arange(row_count) < BLOCK)[None, :, None]
+    own = jnp.broadcast_to(own, (2, row_count, BLOCK))
+    fresh = jnp.ones((2, row_count, row_count - BLOCK), bool)
+    older = jnp.stack([jnp.zeros_like(kept), kept])[:, None, :]
+    older = jnp.broadcast_to(older, (2, row_count, kept.shape[0]))
+    rest = jnp.zeros((2, row_count, EXTRA - row_count - kept.shape[0]), bool)
+    xmask = jnp.where(jnp.concatenate([own, fresh, older, rest], axis=2), 0.0, -1e30)
+    xmask = jnp.tile(xmask.astype(jnp.float32), (1, GROUP, 1))
+
+    def extras(new):
+        again = jnp.broadcast_to(new[:1, BLOCK:], (2, row_count - BLOCK, new.shape[2]))
+        joined = jnp.concatenate([new, again], axis=1)
+        return jnp.pad(joined, ((0, 0), (0, EXTRA - joined.shape[1]), (0, 0)))
+
+    wide = GROUP * HD
+    return pl.pallas_call(
+        attention_kernel,
+        grid=(KVH,),
+        in_specs=[
+            pl.BlockSpec((2, row_count, wide), lambda j: (0, 0, j)),
+            pl.BlockSpec((slots, HD), lambda j: (0, j)),
+            pl.BlockSpec((slots, HD), lambda j: (0, j)),
+            pl.BlockSpec((2, EXTRA, HD), lambda j: (0, 0, j)),
+            pl.BlockSpec((2, EXTRA, HD), lambda j: (0, 0, j)),
+            pl.BlockSpec((2, 1, slots), lambda j: (0, 0, 0)),
+            pl.BlockSpec((2, GROUP * row_count, EXTRA), lambda j: (0, 0, 0)),
+        ],
+        out_specs=pl.BlockSpec((2, row_count, wide), lambda j: (0, 0, j)),
+        out_shape=jax.ShapeDtypeStruct((2, row_count, H * HD), jnp.float32),
+        compiler_params=pltpu.CompilerParams(vmem_limit_bytes=40 * 2**20),
+        name="attention",
+    )(queries, keys, values, extras(new_keys), extras(new_values), mask, xmask)
+
+
+def swapped(i):
+    return (i // 4 % 2) * 8 + (i // 8) * 4 + i % 4
+
+
+SLOTS = 32
+
+
+def expert_kernel(
+    base, tables, gain, wg_in, wu_in, wd_in, out,
+    rows, part, hidden, from_core, from_b, from_a, from_z, residual, carried, wg, wu, wd,
+    w_sem, ag_send, ag_recv, rs_send, rs_recv,
+):
+    y, e = lax.axis_index("rep"), lax.axis_index("exp")
+    c, x, z = lax.rem(e, 2), lax.rem(lax.div(e, 2), 2), lax.div(e, 4)
+    z_low, z_high = lax.rem(z, 2), lax.div(z, 2)
+
+    def device(y_, z_, x_, c_):
+        return (y_, (z_ * 2 + x_) * 2 + c_)
+
+    core = device(y, z, x, 1 - c)
+    a_side = device(y + c * (1 - 2 * y), z, x + (1 - c) * (1 - 2 * x), c)
+    b_side = device(y + (1 - c) * (1 - 2 * y), z, x + c * (1 - 2 * x), c)
+    z_side = [None] + [
+        device(
+            y,
+            ((1 - z_high) if k & 2 else z_high) * 2 + ((1 - z_low) if k & 1 else z_low),
+            x,
+            c,
+        )
+        for k in (1, 2, 3)
+    ]
+
+    loads = [
+        pltpu.make_async_copy(src, dst, w_sem.at[i])
+        for i, (src, dst) in enumerate(((wg_in, wg), (wu_in, wu), (wd_in, wd)))
+    ]
+    for load in loads:
+        load.start()
+
+    barrier = pltpu.get_barrier_semaphore()
+    for peer in (core, a_side, b_side, *z_side[1:]):
+        pl.semaphore_signal(barrier, inc=1, device_id=peer, device_id_type=pl.DeviceIdType.MESH)
+    pl.semaphore_wait(barrier, 6)
+
+    def remote(src, dst, send, recv, peer):
+        return pltpu.make_async_remote_copy(
+            src_ref=src,
+            dst_ref=dst,
+            send_sem=send,
+            recv_sem=recv,
+            device_id=peer,
+            device_id_type=pl.DeviceIdType.MESH,
+        )
+
+    def gather_copy(d):
+        if d < 4:
+            src, peer = 0, z_side[d]
+        elif d < 8:
+            src, peer = d - 4, a_side
+        elif d < 16:
+            src, peer = d - 8, b_side
+        else:
+            src, peer = swapped(d - 16), core
+        return remote(rows.at[src], rows.at[d], ag_send.at[d], ag_recv.at[d], peer)
+
+    def core_copy(j):
+        return remote(
+            part.at[16 + swapped(j)], from_core.at[j], rs_send.at[j], rs_recv.at[j], core
+        )
+
+    def b_copy(j):
+        return remote(
+            part.at[8 + j], from_b.at[j], rs_send.at[16 + j], rs_recv.at[16 + j], b_side
+        )
+
+    def a_copy(j):
+        return remote(
+            part.at[4 + j], from_a.at[j], rs_send.at[24 + j], rs_recv.at[24 + j], a_side
+        )
+
+    def z_copy(k):
+        return remote(
+            part.at[k], from_z.at[k], rs_send.at[28 + k], rs_recv.at[28 + k], z_side[k]
+        )
+
+    width = wd.shape[1]
+    tile = 256
+    row_count = rows.shape[1]
+    half = 16 * row_count
+
+    def experts(which):
+        span = pl.ds(which * 16, 16)
+        share = rows[span, :, width:].reshape(half, rows.shape[2] - width).astype(jnp.float32)
+        lane = lax.broadcasted_iota(jnp.int32, share.shape, 1)
+        share = jnp.sum(jnp.where(lane == e, share, 0.0), axis=1, keepdims=True)
+
+        def up_tile(n, _):
+            columns = pl.ds(pl.multiple_of(n * tile, tile), tile)
+            x_rows = rows[span, :, :width].reshape(half, width)
+            gate = jnp.dot(x_rows, wg[:, columns], preferred_element_type=jnp.float32)
+            up = jnp.dot(x_rows, wu[:, columns], preferred_element_type=jnp.float32)
+            act = gate / (1.0 + jnp.exp(-gate)) * up * share
+            hidden[:, columns] = act.astype(jnp.bfloat16)
+            return 0
+
+        lax.fori_loop(0, hidden.shape[1] // tile, up_tile, 0)
+
+        def down_tile(n, _):
+            columns = pl.ds(pl.multiple_of(n * tile, tile), tile)
+            made = jnp.dot(hidden[...], wd[:, columns], preferred_element_type=jnp.float32)
+            part[span, :, columns] = made.astype(jnp.bfloat16).reshape(16, row_count, tile)
+            return 0
+
+        lax.fori_loop(0, width // tile, down_tile, 0)
+
+    carried[...] = jnp.zeros_like(carried)
+
+    def one_step(step, _):
+        residual[...] = base[step]
+        residual[:BLOCK] = residual[:BLOCK] + carried[...]
+        held = residual[...]
+        inverse = lax.rsqrt(jnp.mean(held * held, axis=1, keepdims=True) + 1e-06)
+        rows[0, :, :width] = (held * inverse * gain[...]).astype(jnp.bfloat16)
+        rows[0, :, width:] = tables[step]
+
+        for d in (1, 2, 3, 4, 8, 16):
+            gather_copy(d).start()
+        for d in (1, 4, 2, 8, 3, 5, 9, 6, 10, 7, 11, 12, 13, 14, 15):
+            gather_copy(d).wait_recv()
+            if d < 4:
+                gather_copy(4 + d).start()
+            if d < 8:
+                gather_copy(8 + d).start()
+            gather_copy(16 + swapped(d)).start()
+        for d in range(16, SLOTS):
+            gather_copy(d).wait_recv()
+        for d in range(1, SLOTS):
+            gather_copy(d).wait_send()
+
+        @pl.when(step == 0)
+        def _():
+            for load in loads:
+                load.wait()
+
+        experts(1)
+        order = (12, 13, 14, 15, 8, 9, 10, 11, 4, 5, 6, 7, 1, 2, 3, 0)
+        for j in order:
+            core_copy(j).start()
+        experts(0)
+        for j in order:
+            core_copy(j).wait_recv()
+            total = part[j].astype(jnp.float32) + from_core[j].astype(jnp.float32)
+            if j < 8:
+                b_copy(j).wait_recv()
+                total = total + from_b[j].astype(jnp.float32)
+            if j < 4:
+                a_copy(j).wait_recv()
+                total = total + from_a[j].astype(jnp.float32)
+            if j > 0:
+                part[j] = total.astype(jnp.bfloat16)
+                (b_copy(j - 8) if j >= 8 else a_copy(j - 4) if j >= 4 else z_copy(j)).start()
+            else:
+                for k in (1, 2, 3):
+                    z_copy(k).wait_recv()
+                    total = total + from_z[k].astype(jnp.float32)
+                result = (residual[...] + total).astype(jnp.bfloat16)
+                out[step] = result
+                carried[...] = result.astype(jnp.float32)[:BLOCK]
+        for j in range(16):
+            core_copy(j).wait_send()
+        for j in range(8):
+            b_copy(j).wait_send()
+        for j in range(4):
+            a_copy(j).wait_send()
+        for k in (1, 2, 3):
+            z_copy(k).wait_send()
+        return 0
+
+    lax.fori_loop(0, 2, one_step, 0)
+
+
+def on_device_close(
+    cache_keys, cache_values, lengths, drift_rows, block_in, drift_in, queries, new_keys,
+    new_values, norm_gain, expert_ids, gate_weights, w_gate, w_up, w_down,
+):
+    attended = attend_both(
+        cache_keys[0],
+        cache_values[0],
+        lengths[0],
+        drift_rows[:, 0],
+        queries[:, 0],
+        new_keys[:, 0],
+        new_values[:, 0],
+    )
+    row_count, width = queries.shape[2], queries.shape[3]
+    first = jnp.stack([block_in[0], jnp.zeros_like(block_in[0])])
+    base = attended + jnp.concatenate([first, drift_in[:, 0]], axis=1).astype(jnp.float32)
+    member = expert_ids[:, 0, :, :, None] == jnp.arange(128)
+    tables = jnp.sum(jnp.where(member, gate_weights[:, 0, :, :, None], 0), axis=2)
+    tables = tables.astype(jnp.bfloat16)
+    vmem = pl.BlockSpec(memory_space=pltpu.VMEM)
+    hbm = pl.BlockSpec(memory_space=pl.ANY)
+    block = (row_count, width)
+    bf16 = jnp.bfloat16
+    out = pl.pallas_call(
+        expert_kernel,
+        out_shape=jax.ShapeDtypeStruct((2, row_count, width), bf16),
+        in_specs=[vmem, vmem, vmem, hbm, hbm, hbm],
+        out_specs=vmem,
+        scratch_shapes=[
+            pltpu.VMEM((SLOTS, row_count, width + 128), bf16),
+            pltpu.VMEM((SLOTS, *block), bf16),
+            pltpu.VMEM((16 * row_count, w_down.shape[1]), bf16),
+            pltpu.VMEM((16, *block), bf16),
+            pltpu.VMEM((8, *block), bf16),
+            pltpu.VMEM((4, *block), bf16),
+            pltpu.VMEM((4, *block), bf16),
+            pltpu.VMEM(block, jnp.float32),
+            pltpu.VMEM((BLOCK, width), jnp.float32),
+            pltpu.VMEM(w_gate.shape[1:], bf16),
+            pltpu.VMEM(w_up.shape[1:], bf16),
+            pltpu.VMEM(w_down.shape[1:], bf16),
+            pltpu.SemaphoreType.DMA((3,)),
+            pltpu.SemaphoreType.DMA((SLOTS,)),
+            pltpu.SemaphoreType.DMA((SLOTS,)),
+            pltpu.SemaphoreType.DMA((SLOTS,)),
+            pltpu.SemaphoreType.DMA((SLOTS,)),
+        ],
+        compiler_params=pltpu.CompilerParams(
+            collective_id=0, has_side_effects=True, vmem_limit_bytes=48 * 2**20
+        ),
+        name="experts",
+    )(base, tables, norm_gain[None], w_gate[0], w_up[0], w_down[0])
+    return out[:, None]
+
+
 def solution(mesh):
+    close = mesh.shape["rep"] == 2 and mesh.shape["exp"] == 16
     placed = (
         P(("rep", "exp"), None, None),
         P(("rep", "exp"), None, None),
@@ -163,7 +476,7 @@
         P("exp", "rep", None),
     )
     return jax.shard_map(
-        on_device,
+        on_device_close if close else on_device,
         mesh=mesh,
         in_specs=placed,
         out_specs=P(None, ("rep", "exp"), None, None),

time: 493 us -> 159 us (0.32)
  blocking collectives: 259 us -> 0 us
  Pallas kernels: 0 us -> 146 us
  waiting for transfers between devices: 76 us -> 0 us
  local copies, waits for them, and re-layouts: 72.4 us -> 9.59 us
  matrix products: 55.7 us -> 0 us
  between operations: 14.9 us -> 0.77 us
  starting transfers between devices: 5.31 us -> 0 us
  other arithmetic: 7.2 us -> 2.15 us
    all_to_all x3 -> x0, blocking collectives: 226 us -> none  [the longest x2 151 us: on_device(): lax.all_to_all(dispatched, 'exp', split_axis=0, concat_axis=0, tiled=True)]
    pallas_call x0 -> x2, Pallas kernels: none -> 146 us  [the longest x1 139 us: on_device_close(): pl.pallas_call(expert_kernel, out_shape=jax.ShapeDtypeStruct((2, row_coun...]
    dot_general x16 -> x0, matrix products: 55.7 us -> none  [the longest x2 18.8 us: expert_terms(): jnp.dot(hidden, down_part, preferred_element_type=jnp.float32)]
    all_to_all x1 -> x0, waiting for transfers between devices: 46.3 us -> none  [on_device(): lax.all_to_all(produced, 'exp', split_axis=0, concat_axis=0, tiled=True)]
    reshape x14 -> x0, local copies, waits for them, and re-layouts: 44.6 us -> none  [the longest x4 23.7 us: expert_terms(): return produced.reshape(routed_rows.shape)]
    all_gather x4 -> x0, blocking collectives: 33 us -> none  [the longest x2 22.9 us: on_device(): lax.all_gather(normed, 'rep', axis=0, tiled=True)]
    reduce_scatter x2 -> x0, waiting for transfers between devices: 29.7 us -> none  [on_device(): lax.psum_scatter(combined.reshape(rep_count * row_count, -1).astype(jnp.b...]
    scatter x4 -> x0, local copies, waits for them, and re-layouts: 9.75 us -> none  [the longest x2 6 us: on_device(): key_rows.at[drift_rows[denoise, 0]].set(new_keys[denoise, 0, BLOCK:])]
  transfers between devices with their start and end apart: 3 -> 0, of which waited for: 3 -> 0; matrix products, arithmetic and copies ran while one was open for 3% -> 0% of each run, Pallas kernels for 0% -> 0%
where the time goes in v1:
time: 159 us; the launch traced here: 158 us
  Pallas kernels  146 us (92%)
  local copies, waits for them, and re-layouts  9.59 us (6%)
  other arithmetic  2.15 us (1%)
    pallas_call x1, Pallas kernels, on_device_close(): pl.pallas_call(expert_kernel, out_shape=jax.ShapeDtypeStruct((2, row_coun...  139 us
    unnamed x19, local copies, waits for them, and re-layouts  7.03 us
    pallas_call x1, Pallas kernels, attend_both(): pl.pallas_call(attention_kernel, grid=(KVH,), in_specs=[pl.BlockSpec((2,...  6.25 us

profile of v1, /device:TPU:0, one launch (start us, length us, event | category | flops | bytes accessed | tf_op | source)
XLA Modules:
  0.0 158.1 jit_solution(11663592310397066139)
XLA Ops:
  0.0 0.0 copy-start.5
  0.0 0.0 copy-start.6
  0.0 0.0 copy-start.7
  0.0 0.0 copy-start.8
  0.0 0.0 copy-start.4
  0.0 0.7 slice_bitcast_fusion.1
  0.8 0.7 slice_bitcast_fusion
  1.5 0.8 fusion.6
  2.3 0.7 slice_bitcast_fusion.3
  3.0 0.2 compare_reduce_fusion
  3.2 0.1 broadcast_in_dim.77
  3.3 0.1 pad.14.clone
  3.4 0.1 pad.16.clone
  3.4 0.1 add_select_fusion.1
  3.5 0.8 fusion.8
  5.1 0.0 copy-start.1
  5.1 1.6 %copy-done.1 = bf16[1,2048,512]{2,1,0:T(8,128)(2,1)S(1)} copy-done((bf16[1,2048,512]{2,1,0:T(8,128)(2,1)S(1)}, bf16[1,2048,512]{2,1,0:T(8,128)(2,1)}, u32[]{:S(2)}) %copy-start.1) | copy-done | bytes 2097176
  6.7 0.0 copy-start.2
  6.7 1.6 %copy-done.2 = bf16[1,2048,512]{2,1,0:T(8,128)(2,1)S(1)} copy-done((bf16[1,2048,512]{2,1,0:T(8,128)(2,1)S(1)}, bf16[1,2048,512]{2,1,0:T(8,128)(2,1)}, u32[]{:S(2)}) %copy-start.2) | copy-done | bytes 2097176
  8.2 0.0 copy-start.3
  8.3 0.9 copy-done.3
  9.2 6.2 %attention.1 = f32[2,16,4096]{2,1,0:T(8,128)S(1)} custom-call(bf16[2,16,4096]{2,1,0:T(8,128)(2,1)S(1)} %bitcast.38, bf16[2048,512]{1,0:T(8,128)(2,1)S(1)} %bitcast.34, bf16[2048,512]{1,0:T(8,128)(2,1)S(1)} %bitcast.35, bf16[2,128,512]{2,1,0:T(8,128)(2,1)S(1)} %get-tuple-element.9.xk_ref, bf16[2,128,512]{2,1,0:T(8,128)(2,1)S(1)} %get-tuple-element.10.xv_ref, ...), custom_call_target="tpu_custom_call" | custom-call | tf_op jit(solution)/shard_map/attention/pallas_call | solution.py:204
  15.5 0.0 copy-done.5
  15.5 0.0 copy-done.6
  15.5 0.0 copy-done.7
  15.5 0.1 copy.19
  15.6 0.0 copy-done.8
  15.6 0.1 copy.20
  15.7 0.2 fusion.10.tables
  15.9 0.0 copy-done.4
  15.9 0.0 copy-start
  15.9 2.2 %copy-done = bf16[1,4096,512]{2,1,0:T(8,128)(2,1)S(1)} copy-done((bf16[1,4096,512]{2,1,0:T(8,128)(2,1)S(1)}, bf16[1,4096,512]{2,1,0:T(8,128)(2,1)}, u32[]{:S(2)}) %copy-start) | copy-done | bytes 4194328
  18.1 139.4 %experts.1 = bf16[2,16,4096]{2,1,0:T(8,128)(2,1)S(1)} custom-call(f32[2,16,4096]{2,1,0:T(8,128)S(1)} %convert_add_fusion.base, bf16[2,16,128]{2,1,0:T(8,128)(2,1)S(1)} %fusion.10.tables, f32[1,4096]{1,0:T(1,128)S(1)} %bitcast.39, bf16[4096,512]{1,0:T(8,128)(2,1)S(1)} %bitcast.33, bf16[4096,512]{1,0:T(8,128)(2,1)} %bitcast.40, bf16[512,4096]{1,0:T(8,128)(2,1)} %bitcast.41), custom_call_target="tpu_custom_call" | custom-call | tf_op jit(solution)/shard_map/experts/pallas_call | solution.py:427
  157.4 0.7 copy.24
  (12 shorter events, 0.2 us)
Async XLA Ops:
  0.0 15.5 %copy-start.5 = (bf16[2,1,8,4096]{3,2,1,0:T(8,128)(2,1)S(1)}, bf16[2,1,8,4096]{3,2,1,0:T(8,128)(2,1)}, u32[]{:S(2)}) copy-start(bf16[2,1,8,4096]{3,2,1,0:T(8,128)(2,1)} %param.20) | copy-start | bytes 393220
  0.0 15.5 %copy-start.6 = (bf16[1,8,4096]{2,1,0:T(8,128)(2,1)S(1)}, bf16[1,8,4096]{2,1,0:T(8,128)(2,1)}, u32[]{:S(2)}) copy-start(bf16[1,8,4096]{2,1,0:T(8,128)(2,1)} %param.19) | copy-start | bytes 196612
  0.0 15.5 %copy-start.7 = (s32[2,1,16,8]{2,3,1,0:T(8,128)S(1)}, s32[2,1,16,8]{2,3,1,0:T(8,128)}, u32[]{:S(2)}) copy-start(s32[2,1,16,8]{2,3,1,0:T(8,128)} %param.25) | copy-start | bytes 3076
  0.0 15.6 %copy-start.8 = (bf16[2,1,16,8]{2,3,1,0:T(8,128)(2,1)S(1)}, bf16[2,1,16,8]{2,3,1,0:T(8,128)(2,1)}, u32[]{:S(2)}) copy-start(bf16[2,1,16,8]{2,3,1,0:T(8,128)(2,1)} %param.26) | copy-start | bytes 1540
  0.0 15.8 %copy-start.4 = (f32[4096]{0:T(1024)S(1)}, f32[4096]{0:T(1024)}, u32[]{:S(2)}) copy-start(f32[4096]{0:T(1024)} %param.24) | copy-start | bytes 49156
  5.1 1.6 %copy-start.1 = (bf16[1,2048,512]{2,1,0:T(8,128)(2,1)S(1)}, bf16[1,2048,512]{2,1,0:T(8,128)(2,1)}, u32[]{:S(2)}) copy-start(bf16[1,2048,512]{2,1,0:T(8,128)(2,1)} %param.15) | copy-start | bytes 6291460
  6.7 1.6 %copy-start.2 = (bf16[1,2048,512]{2,1,0:T(8,128)(2,1)S(1)}, bf16[1,2048,512]{2,1,0:T(8,128)(2,1)}, u32[]{:S(2)}) copy-start(bf16[1,2048,512]{2,1,0:T(8,128)(2,1)} %param.16) | copy-start | bytes 6291460
  8.2 0.9 copy-start.3
  15.9 2.2 %copy-start = (bf16[1,4096,512]{2,1,0:T(8,128)(2,1)S(1)}, bf16[1,4096,512]{2,1,0:T(8,128)(2,1)}, u32[]{:S(2)}) copy-start(bf16[1,4096,512]{2,1,0:T(8,128)(2,1)} %param.27) | copy-start | bytes 12582916

commit v2 on v1

--- a/solution.py
+++ b/solution.py
@@ -215,13 +215,9 @@
         ],
         out_specs=pl.BlockSpec((2, row_count, wide), lambda j: (0, 0, j)),
         out_shape=jax.ShapeDtypeStruct((2, row_count, H * HD), jnp.float32),
-        compiler_params=pltpu.CompilerParams(vmem_limit_bytes=40 * 2**20),
+        compiler_params=pltpu.CompilerParams(vmem_limit_bytes=60 * 2**20),
         name="attention",
     )(queries, keys, values, extras(new_keys), extras(new_values), mask, xmask)
-
-
-def swapped(i):
-    return (i // 4 % 2) * 8 + (i // 8) * 4 + i % 4
 
 
 SLOTS = 32
@@ -279,20 +275,19 @@
             src, peer = 0, z_side[d]
         elif d < 8:
             src, peer = d - 4, a_side
-        elif d < 16:
-            src, peer = d - 8, b_side
+        elif d < 16 or d >= 24:
+            src, peer = d - 8, core
         else:
-            src, peer = swapped(d - 16), core
+            src, peer = d - 16, b_side
         return remote(rows.at[src], rows.at[d], ag_send.at[d], ag_recv.at[d], peer)
 
     def core_copy(j):
-        return remote(
-            part.at[16 + swapped(j)], from_core.at[j], rs_send.at[j], rs_recv.at[j], core
-        )
+        src = 8 + j if j < 8 else 16 + j
+        return remote(part.at[src], from_core.at[j], rs_send.at[j], rs_recv.at[j], core)
 
     def b_copy(j):
         return remote(
-            part.at[8 + j], from_b.at[j], rs_send.at[16 + j], rs_recv.at[16 + j], b_side
+            part.at[16 + j], from_b.at[j], rs_send.at[16 + j], rs_recv.at[16 + j], b_side
         )
 
     def a_copy(j):
@@ -310,30 +305,32 @@
     row_count = rows.shape[1]
     half = 16 * row_count
 
-    def experts(which):
-        span = pl.ds(which * 16, 16)
+    def up_tile(first, n):
+        span = pl.ds(first, 16)
         share = rows[span, :, width:].reshape(half, rows.shape[2] - width).astype(jnp.float32)
         lane = lax.broadcasted_iota(jnp.int32, share.shape, 1)
         share = jnp.sum(jnp.where(lane == e, share, 0.0), axis=1, keepdims=True)
-
-        def up_tile(n, _):
-            columns = pl.ds(pl.multiple_of(n * tile, tile), tile)
-            x_rows = rows[span, :, :width].reshape(half, width)
-            gate = jnp.dot(x_rows, wg[:, columns], preferred_element_type=jnp.float32)
-            up = jnp.dot(x_rows, wu[:, columns], preferred_element_type=jnp.float32)
-            act = gate / (1.0 + jnp.exp(-gate)) * up * share
-            hidden[:, columns] = act.astype(jnp.bfloat16)
+        columns = pl.ds(n * tile, tile)
+        x_rows = rows[span, :, :width].reshape(half, width)
+        gate = jnp.dot(x_rows, wg[:, columns], preferred_element_type=jnp.float32)
+        up = jnp.dot(x_rows, wu[:, columns], preferred_element_type=jnp.float32)
+        act = gate / (1.0 + jnp.exp(-gate)) * up * share
+        hidden[:, columns] = act.astype(jnp.bfloat16)
+
+    def down(first, offset):
+        span = pl.ds(first, 8)
+
+        def down_tile(n, _):
+            columns = pl.ds(pl.multiple_of(n * 512, 512), 512)
+            made = jnp.dot(
+                hidden[pl.ds(offset, half // 2)],
+                wd[:, columns],
+                preferred_element_type=jnp.float32,
+            )
+            part[span, :, columns] = made.astype(jnp.bfloat16).reshape(8, row_count, 512)
             return 0
 
-        lax.fori_loop(0, hidden.shape[1] // tile, up_tile, 0)
-
-        def down_tile(n, _):
-            columns = pl.ds(pl.multiple_of(n * tile, tile), tile)
-            made = jnp.dot(hidden[...], wd[:, columns], preferred_element_type=jnp.float32)
-            part[span, :, columns] = made.astype(jnp.bfloat16).reshape(16, row_count, tile)
-            return 0
-
-        lax.fori_loop(0, width // tile, down_tile, 0)
+        lax.fori_loop(0, width // 512, down_tile, 0)
 
     carried[...] = jnp.zeros_like(carried)
 
@@ -345,33 +342,52 @@
         rows[0, :, :width] = (held * inverse * gain[...]).astype(jnp.bfloat16)
         rows[0, :, width:] = tables[step]
 
-        for d in (1, 2, 3, 4, 8, 16):
+        for d in (16, 4, 1, 2, 3, 8):
             gather_copy(d).start()
-        for d in (1, 4, 2, 8, 3, 5, 9, 6, 10, 7, 11, 12, 13, 14, 15):
+        for d in (1, 4, 2, 3, 5, 6, 7):
             gather_copy(d).wait_recv()
+            gather_copy(16 + d).start()
             if d < 4:
                 gather_copy(4 + d).start()
-            if d < 8:
+            gather_copy(8 + d).start()
+
+        def pass_on(*slots):
+            for d in slots:
+                gather_copy(d).wait_recv()
                 gather_copy(8 + d).start()
-            gather_copy(16 + swapped(d)).start()
-        for d in range(16, SLOTS):
-            gather_copy(d).wait_recv()
-        for d in range(1, SLOTS):
-            gather_copy(d).wait_send()
 
         @pl.when(step == 0)
         def _():
             for load in loads:
                 load.wait()
 
-        experts(1)
-        order = (12, 13, 14, 15, 8, 9, 10, 11, 4, 5, 6, 7, 1, 2, 3, 0)
-        for j in order:
+        for d in range(8, 16):
+            gather_copy(d).wait_recv()
+        up_tile(0, 0)
+        pass_on(16, 17)
+        up_tile(0, 1)
+        pass_on(18, 20)
+        down(8, half // 2)
+        for j in range(8):
             core_copy(j).start()
-        experts(0)
-        for j in order:
+        pass_on(19, 21)
+        down(0, 0)
+        pass_on(22, 23)
+        for d in range(24, SLOTS):
+            gather_copy(d).wait_recv()
+        up_tile(16, 0)
+        up_tile(16, 1)
+        for d in range(1, SLOTS):
+            gather_copy(d).wait_send()
+        down(24, half // 2)
+        far = (12, 13, 14, 15, 8, 9, 10, 11)
+        for j in far:
+            core_copy(j).start()
+        down(16, 0)
+        for j in (*far, 4, 5, 6, 7, 1, 2, 3, 0):
+            mine = j if j < 8 else 8 + j
             core_copy(j).wait_recv()
-            total = part[j].astype(jnp.float32) + from_core[j].astype(jnp.float32)
+            total = part[mine].astype(jnp.float32) + from_core[j].astype(jnp.float32)
             if j < 8:
                 b_copy(j).wait_recv()
                 total = total + from_b[j].astype(jnp.float32)
@@ -379,7 +395,7 @@
                 a_copy(j).wait_recv()
                 total = total + from_a[j].astype(jnp.float32)
             if j > 0:
-                part[j] = total.astype(jnp.bfloat16)
+                part[mine] = total.astype(jnp.bfloat16)
                 (b_copy(j - 8) if j >= 8 else a_copy(j - 4) if j >= 4 else z_copy(j)).start()
             else:
                 for k in (1, 2, 3):
@@ -449,7 +465,7 @@
             pltpu.SemaphoreType.DMA((SLOTS,)),
         ],
         compiler_params=pltpu.CompilerParams(
-            collective_id=0, has_side_effects=True, vmem_limit_bytes=48 * 2**20
+            collective_id=0, has_side_effects=True, vmem_limit_bytes=60 * 2**20
         ),
         name="experts",
     )(base, tables, norm_gain[None], w_gate[0], w_up[0], w_down[0])

time: 159 us -> 152 us (0.956)
  Pallas kernels: 146 us -> 140 us
  local copies, waits for them, and re-layouts: 9.59 us -> 4.89 us
  other arithmetic: 2.15 us -> 5.97 us
    pallas_call x1, Pallas kernels: 139 us -> 132 us  [on_device_close(): pl.pallas_call(expert_kernel, out_shape=jax.ShapeDtypeStruct((2, row_coun...]
    unnamed x19 -> x9, local copies, waits for them, and re-layouts: 7.03 us -> 1.68 us
    add x1, other arithmetic: 0.04 us -> 1.87 us  [on_device_close(): attended + jnp.concatenate([first, drift_in[:, 0]], axis=1).astype(jnp.fl...]
where the time goes in v2:
time: 152 us; the launch traced here: 151 us
  Pallas kernels  140 us (92%)
  other arithmetic  5.97 us (4%)
  local copies, waits for them, and re-layouts  4.89 us (3%)
    pallas_call x1, Pallas kernels, on_device_close(): pl.pallas_call(expert_kernel, out_shape=jax.ShapeDtypeStruct((2, row_coun...  132 us
    pallas_call x1, Pallas kernels, attend_both(): pl.pallas_call(attention_kernel, grid=(KVH,), in_specs=[pl.BlockSpec((2,...  7.64 us

profile of v2, /device:TPU:0, one launch (start us, length us, event | category | flops | bytes accessed | tf_op | source)
XLA Modules:
  0.0 151.4 jit_solution(10417696710040637360)
XLA Ops:
  0.0 0.0 copy-start
  0.0 0.0 copy-start.1
  0.0 0.0 copy-start.2
  0.0 0.0 copy-start.3
  0.0 0.7 slice_bitcast_fusion.1
  0.8 0.7 slice_bitcast_fusion
  1.5 1.6 %fusion.6 = (bf16[2,128,512]{2,1,0:T(8,128)(2,1)}, bf16[2,128,512]{2,1,0:T(8,128)(2,1)}) fusion(bf16[2,8,512]{2,1,0:T(8,128)(2,1)S(1)} %broadcast_in_dim.72, bf16[2,16,512]{2,1,0:T(8,128)(2,1)} %bitcast.43, bf16[2,8,512]{2,1,0:T(8,128)(2,1)S(1)} %broadcast_in_dim.74, bf16[2,16,512]{2,1,0:T(8,128)(2,1)} %bitcast.45), kind=kLoop, calls=%fused_computation.9 | loop fusion | flops 1703936 | bytes 622592 | tf_op jit(solution)/shard_map/concatenate | solution.py:200
  3.1 0.7 slice_bitcast_fusion.3
  3.7 0.2 compare_reduce_fusion
  4.0 0.1 broadcast_in_dim.77
  4.0 0.1 pad.14.clone
  4.1 0.1 pad.16.clone
  4.2 0.1 add_select_fusion.1
  4.3 0.7 tile.4
  5.0 0.8 fusion.8
  6.4 0.6 add_select_fusion.mask_ref
  7.1 7.6 %attention.1 = f32[2,16,4096]{2,1,0:T(8,128)} custom-call(bf16[2,16,4096]{2,1,0:T(8,128)(2,1)} %bitcast.40, bf16[2048,512]{1,0:T(8,128)(2,1)} %bitcast.36, bf16[2048,512]{1,0:T(8,128)(2,1)} %bitcast.37, bf16[2,128,512]{2,1,0:T(8,128)(2,1)} %get-tuple-element.9.xk_ref, bf16[2,128,512]{2,1,0:T(8,128)(2,1)} %get-tuple-element.10.xv_ref, ...), custom_call_target="tpu_custom_call" | custom-call | tf_op jit(solution)/shard_map/attention/pallas_call | solution.py:204
  14.7 0.0 copy-done
  14.7 0.0 copy-done.1
  14.7 1.9 %convert_add_fusion.base = f32[2,16,4096]{2,1,0:T(8,128)} fusion(f32[2,16,4096]{2,1,0:T(8,128)} %attention.1, bf16[1,8,4096]{2,1,0:T(8,128)(2,1)S(1)} %copy-done.1, bf16[2,8,4096]{2,1,0:T(8,128)(2,1)S(1)} %bitcast.41), kind=kLoop, calls=%fused_computation.6 | loop fusion | flops 917504 | bytes 1245184 | tf_op jit(solution)/shard_map/add | solution.py:435
  16.6 0.0 copy-done.2
  16.6 0.1 copy.19
  16.7 0.0 copy-done.3
  16.7 0.1 copy.20
  16.8 0.8 fusion.10.tables
  17.5 132.2 %experts.1 = bf16[2,16,4096]{2,1,0:T(8,128)(2,1)} custom-call(f32[2,16,4096]{2,1,0:T(8,128)} %convert_add_fusion.base, bf16[2,16,128]{2,1,0:T(8,128)(2,1)} %fusion.10.tables, f32[1,4096]{1,0:T(1,128)} %bitcast.46, bf16[4096,512]{1,0:T(8,128)(2,1)} %bitcast.33, bf16[4096,512]{1,0:T(8,128)(2,1)} %bitcast.34, bf16[512,4096]{1,0:T(8,128)(2,1)} %bitcast.35), custom_call_target="tpu_custom_call" | custom-call | tf_op jit(solution)/shard_map/experts/pallas_call | solution.py:443
  149.7 1.7 %copy.24 = bf16[2,1,16,4096]{3,2,1,0:T(8,128)(2,1)} copy(bf16[2,1,16,4096]{3,2,1,0:T(8,128)(2,1)} %bitcast.38) | data formatting | bytes 524288
  (9 shorter events, 0.1 us)
Async XLA Ops:
  0.0 14.7 %copy-start = (bf16[2,1,8,4096]{3,2,1,0:T(8,128)(2,1)S(1)}, bf16[2,1,8,4096]{3,2,1,0:T(8,128)(2,1)}, u32[]{:S(2)}) copy-start(bf16[2,1,8,4096]{3,2,1,0:T(8,128)(2,1)} %param.20) | copy-start | bytes 393220
  0.0 14.7 %copy-start.1 = (bf16[1,8,4096]{2,1,0:T(8,128)(2,1)S(1)}, bf16[1,8,4096]{2,1,0:T(8,128)(2,1)}, u32[]{:S(2)}) copy-start(bf16[1,8,4096]{2,1,0:T(8,128)(2,1)} %param.19) | copy-start | bytes 196612
  0.0 16.6 %copy-start.2 = (s32[2,1,16,8]{2,3,1,0:T(8,128)S(1)}, s32[2,1,16,8]{2,3,1,0:T(8,128)}, u32[]{:S(2)}) copy-start(s32[2,1,16,8]{2,3,1,0:T(8,128)} %param.25) | copy-start | bytes 3076
  0.0 16.7 %copy-start.3 = (bf16[2,1,16,8]{2,3,1,0:T(8,128)(2,1)S(1)}, bf16[2,1,16,8]{2,3,1,0:T(8,128)(2,1)}, u32[]{:S(2)}) copy-start(bf16[2,1,16,8]{2,3,1,0:T(8,128)(2,1)} %param.26) | copy-start | bytes 1540

commit v3 on v2

--- a/solution.py
+++ b/solution.py
@@ -271,34 +271,31 @@
         )
 
     def gather_copy(d):
-        if d < 4:
-            src, peer = 0, z_side[d]
-        elif d < 8:
-            src, peer = d - 4, a_side
-        elif d < 16 or d >= 24:
+        if d & 8:
             src, peer = d - 8, core
+        elif d & 4:
+            src, peer = d - 4, b_side
+        elif d & 2:
+            src, peer = d - 2, a_side
         else:
-            src, peer = d - 16, b_side
+            src, peer = 0, z_side[d // 8 + d % 2]
         return remote(rows.at[src], rows.at[d], ag_send.at[d], ag_recv.at[d], peer)
 
     def core_copy(j):
-        src = 8 + j if j < 8 else 16 + j
-        return remote(part.at[src], from_core.at[j], rs_send.at[j], rs_recv.at[j], core)
+        src = part.at[j // 8 * 16 + 8 + j % 8]
+        return remote(src, from_core.at[j], rs_send.at[j], rs_recv.at[j], core)
 
     def b_copy(j):
-        return remote(
-            part.at[16 + j], from_b.at[j], rs_send.at[16 + j], rs_recv.at[16 + j], b_side
-        )
+        src = part.at[j // 4 * 16 + 4 + j % 4]
+        return remote(src, from_b.at[j], rs_send.at[16 + j], rs_recv.at[16 + j], b_side)
 
     def a_copy(j):
-        return remote(
-            part.at[4 + j], from_a.at[j], rs_send.at[24 + j], rs_recv.at[24 + j], a_side
-        )
+        src = part.at[j // 2 * 16 + 2 + j % 2]
+        return remote(src, from_a.at[j], rs_send.at[24 + j], rs_recv.at[24 + j], a_side)
 
     def z_copy(k):
-        return remote(
-            part.at[k], from_z.at[k], rs_send.at[28 + k], rs_recv.at[28 + k], z_side[k]
-        )
+        src = part.at[k // 2 * 16 + k % 2]
+        return remote(src, from_z.at[k], rs_send.at[28 + k], rs_recv.at[28 + k], z_side[k])
 
     width = wd.shape[1]
     tile = 256
@@ -315,15 +312,15 @@
         gate = jnp.dot(x_rows, wg[:, columns], preferred_element_type=jnp.float32)
         up = jnp.dot(x_rows, wu[:, columns], preferred_element_type=jnp.float32)
         act = gate / (1.0 + jnp.exp(-gate)) * up * share
-        hidden[:, columns] = act.astype(jnp.bfloat16)
-
-    def down(first, offset):
+        hidden[pl.ds(first * row_count, half), columns] = act.astype(jnp.bfloat16)
+
+    def down(first):
         span = pl.ds(first, 8)
 
         def down_tile(n, _):
             columns = pl.ds(pl.multiple_of(n * 512, 512), 512)
             made = jnp.dot(
-                hidden[pl.ds(offset, half // 2)],
+                hidden[pl.ds(first * row_count, half // 2)],
                 wd[:, columns],
                 preferred_element_type=jnp.float32,
             )
@@ -342,19 +339,22 @@
         rows[0, :, :width] = (held * inverse * gain[...]).astype(jnp.bfloat16)
         rows[0, :, width:] = tables[step]
 
-        for d in (16, 4, 1, 2, 3, 8):
-            gather_copy(d).start()
-        for d in (1, 4, 2, 3, 5, 6, 7):
-            gather_copy(d).wait_recv()
-            gather_copy(16 + d).start()
-            if d < 4:
+        def forward(d):
+            if d & 6 == 0:
+                gather_copy(2 + d).start()
+            if d & 4 == 0:
                 gather_copy(4 + d).start()
             gather_copy(8 + d).start()
 
         def pass_on(*slots):
             for d in slots:
                 gather_copy(d).wait_recv()
-                gather_copy(8 + d).start()
+                forward(d)
+
+        for d in (1, 16, 17):
+            gather_copy(d).start()
+        forward(0)
+        pass_on(2, 1, 4, 3, 5, 16, 6, 18, 7)
 
         @pl.when(step == 0)
         def _():
@@ -364,46 +364,61 @@
         for d in range(8, 16):
             gather_copy(d).wait_recv()
         up_tile(0, 0)
-        pass_on(16, 17)
+        pass_on(17, 20)
         up_tile(0, 1)
-        pass_on(18, 20)
-        down(8, half // 2)
-        for j in range(8):
-            core_copy(j).start()
-        pass_on(19, 21)
-        down(0, 0)
-        pass_on(22, 23)
+        pass_on(19, 22, 21, 23)
         for d in range(24, SLOTS):
             gather_copy(d).wait_recv()
         up_tile(16, 0)
         up_tile(16, 1)
         for d in range(1, SLOTS):
             gather_copy(d).wait_send()
-        down(24, half // 2)
-        far = (12, 13, 14, 15, 8, 9, 10, 11)
-        for j in far:
-            core_copy(j).start()
-        down(16, 0)
-        for j in (*far, 4, 5, 6, 7, 1, 2, 3, 0):
-            mine = j if j < 8 else 8 + j
+
+        def summed(z_half, r):
+            j, mine = z_half * 8 + r, z_half * 16 + r
             core_copy(j).wait_recv()
             total = part[mine].astype(jnp.float32) + from_core[j].astype(jnp.float32)
-            if j < 8:
-                b_copy(j).wait_recv()
-                total = total + from_b[j].astype(jnp.float32)
-            if j < 4:
-                a_copy(j).wait_recv()
-                total = total + from_a[j].astype(jnp.float32)
-            if j > 0:
-                part[mine] = total.astype(jnp.bfloat16)
-                (b_copy(j - 8) if j >= 8 else a_copy(j - 4) if j >= 4 else z_copy(j)).start()
-            else:
-                for k in (1, 2, 3):
-                    z_copy(k).wait_recv()
-                    total = total + from_z[k].astype(jnp.float32)
-                result = (residual[...] + total).astype(jnp.bfloat16)
-                out[step] = result
-                carried[...] = result.astype(jnp.float32)[:BLOCK]
+            if r < 4:
+                b_copy(z_half * 4 + r).wait_recv()
+                total = total + from_b[z_half * 4 + r].astype(jnp.float32)
+            if r < 2:
+                a_copy(z_half * 2 + r).wait_recv()
+                total = total + from_a[z_half * 2 + r].astype(jnp.float32)
+            return total
+
+        def hand_on(z_half, *places):
+            for r in places:
+                part[z_half * 16 + r] = summed(z_half, r).astype(jnp.bfloat16)
+                if r >= 4:
+                    b_copy(z_half * 4 + r - 4).start()
+                elif r >= 2:
+                    a_copy(z_half * 2 + r - 2).start()
+                else:
+                    z_copy(z_half * 2 + r).start()
+
+        order = (7, 5, 6, 4, 3, 1, 2, 0)
+        down(24)
+        for r in order:
+            core_copy(8 + r).start()
+        down(16)
+        hand_on(1, 7, 5, 6, 4)
+        down(8)
+        for r in order:
+            core_copy(r).start()
+        hand_on(1, 3)
+        down(0)
+        hand_on(0, 7, 5)
+        hand_on(1, 2, 1)
+        hand_on(0, 6, 4)
+        hand_on(1, 0)
+        hand_on(0, 3, 2, 1)
+        total = summed(0, 0)
+        for k in (1, 2, 3):
+            z_copy(k).wait_recv()
+            total = total + from_z[k].astype(jnp.float32)
+        result = (residual[...] + total).astype(jnp.bfloat16)
+        out[step] = result
+        carried[...] = result.astype(jnp.float32)[:BLOCK]
         for j in range(16):
             core_copy(j).wait_send()
         for j in range(8):
@@ -448,7 +463,7 @@
         scratch_shapes=[
             pltpu.VMEM((SLOTS, row_count, width + 128), bf16),
             pltpu.VMEM((SLOTS, *block), bf16),
-            pltpu.VMEM((16 * row_count, w_down.shape[1]), bf16),
+            pltpu.VMEM((SLOTS * row_count, w_down.shape[1]), bf16),
             pltpu.VMEM((16, *block), bf16),
             pltpu.VMEM((8, *block), bf16),
             pltpu.VMEM((4, *block), bf16),

time: 152 us -> 142 us (0.934)
  Pallas kernels: 140 us -> 130 us
    pallas_call x1, Pallas kernels: 132 us -> 122 us  [on_device_close(): pl.pallas_call(expert_kernel, out_shape=jax.ShapeDtypeStruct((2, row_coun...]
where the time goes in v3:
time: 142 us; the launch traced here: 141 us
  Pallas kernels  130 us (92%)
  other arithmetic  5.97 us (4%)
  local copies, waits for them, and re-layouts  4.89 us (3%)
    pallas_call x1, Pallas kernels, on_device_close(): pl.pallas_call(expert_kernel, out_shape=jax.ShapeDtypeStruct((2, row_coun...  122 us
    pallas_call x1, Pallas kernels, attend_both(): pl.pallas_call(attention_kernel, grid=(KVH,), in_specs=[pl.BlockSpec((2,...  7.64 us

profile of v3, /device:TPU:0, one launch (start us, length us, event | category | flops | bytes accessed | tf_op | source)
XLA Modules:
  0.0 141.4 jit_solution(12853980290377150292)
XLA Ops:
  0.0 0.0 copy-start
  0.0 0.0 copy-start.1
  0.0 0.0 copy-start.2
  0.0 0.0 copy-start.3
  0.0 0.7 slice_bitcast_fusion.1
  0.8 0.7 slice_bitcast_fusion
  1.5 1.6 %fusion.6 = (bf16[2,128,512]{2,1,0:T(8,128)(2,1)}, bf16[2,128,512]{2,1,0:T(8,128)(2,1)}) fusion(bf16[2,8,512]{2,1,0:T(8,128)(2,1)S(1)} %broadcast_in_dim.72, bf16[2,16,512]{2,1,0:T(8,128)(2,1)} %bitcast.43, bf16[2,8,512]{2,1,0:T(8,128)(2,1)S(1)} %broadcast_in_dim.74, bf16[2,16,512]{2,1,0:T(8,128)(2,1)} %bitcast.45), kind=kLoop, calls=%fused_computation.9 | loop fusion | flops 1703936 | bytes 622592 | tf_op jit(solution)/shard_map/concatenate | solution.py:200
  3.1 0.7 slice_bitcast_fusion.3
  3.7 0.2 compare_reduce_fusion
  4.0 0.1 broadcast_in_dim.77
  4.0 0.1 pad.14.clone
  4.1 0.1 pad.16.clone
  4.2 0.1 add_select_fusion.1
  4.3 0.7 tile.4
  5.0 0.8 fusion.8
  6.4 0.6 add_select_fusion.mask_ref
  7.1 7.6 %attention.1 = f32[2,16,4096]{2,1,0:T(8,128)} custom-call(bf16[2,16,4096]{2,1,0:T(8,128)(2,1)} %bitcast.40, bf16[2048,512]{1,0:T(8,128)(2,1)} %bitcast.36, bf16[2048,512]{1,0:T(8,128)(2,1)} %bitcast.37, bf16[2,128,512]{2,1,0:T(8,128)(2,1)} %get-tuple-element.9.xk_ref, bf16[2,128,512]{2,1,0:T(8,128)(2,1)} %get-tuple-element.10.xv_ref, ...), custom_call_target="tpu_custom_call" | custom-call | tf_op jit(solution)/shard_map/attention/pallas_call | solution.py:204
  14.7 0.0 copy-done
  14.7 0.0 copy-done.1
  14.7 1.9 %convert_add_fusion.base = f32[2,16,4096]{2,1,0:T(8,128)} fusion(f32[2,16,4096]{2,1,0:T(8,128)} %attention.1, bf16[1,8,4096]{2,1,0:T(8,128)(2,1)S(1)} %copy-done.1, bf16[2,8,4096]{2,1,0:T(8,128)(2,1)S(1)} %bitcast.41), kind=kLoop, calls=%fused_computation.6 | loop fusion | flops 917504 | bytes 1245184 | tf_op jit(solution)/shard_map/add | solution.py:450
  16.6 0.0 copy-done.2
  16.6 0.1 copy.19
  16.7 0.0 copy-done.3
  16.7 0.1 copy.20
  16.8 0.8 fusion.10.tables
  17.5 122.3 %experts.1 = bf16[2,16,4096]{2,1,0:T(8,128)(2,1)} custom-call(f32[2,16,4096]{2,1,0:T(8,128)} %convert_add_fusion.base, bf16[2,16,128]{2,1,0:T(8,128)(2,1)} %fusion.10.tables, f32[1,4096]{1,0:T(1,128)} %bitcast.46, bf16[4096,512]{1,0:T(8,128)(2,1)} %bitcast.33, bf16[4096,512]{1,0:T(8,128)(2,1)} %bitcast.34, bf16[512,4096]{1,0:T(8,128)(2,1)} %bitcast.35), custom_call_target="tpu_custom_call" | custom-call | tf_op jit(solution)/shard_map/experts/pallas_call | solution.py:458
  139.8 1.7 %copy.24 = bf16[2,1,16,4096]{3,2,1,0:T(8,128)(2,1)} copy(bf16[2,1,16,4096]{3,2,1,0:T(8,128)(2,1)} %bitcast.38) | data formatting | bytes 524288
  (9 shorter events, 0.1 us)
Async XLA Ops:
  0.0 14.7 %copy-start = (bf16[2,1,8,4096]{3,2,1,0:T(8,128)(2,1)S(1)}, bf16[2,1,8,4096]{3,2,1,0:T(8,128)(2,1)}, u32[]{:S(2)}) copy-start(bf16[2,1,8,4096]{3,2,1,0:T(8,128)(2,1)} %param.20) | copy-start | bytes 393220
  0.0 14.7 %copy-start.1 = (bf16[1,8,4096]{2,1,0:T(8,128)(2,1)S(1)}, bf16[1,8,4096]{2,1,0:T(8,128)(2,1)}, u32[]{:S(2)}) copy-start(bf16[1,8,4096]{2,1,0:T(8,128)(2,1)} %param.19) | copy-start | bytes 196612
  0.0 16.6 %copy-start.2 = (s32[2,1,16,8]{2,3,1,0:T(8,128)S(1)}, s32[2,1,16,8]{2,3,1,0:T(8,128)}, u32[]{:S(2)}) copy-start(s32[2,1,16,8]{2,3,1,0:T(8,128)} %param.25) | copy-start | bytes 3076
  0.0 16.7 %copy-start.3 = (bf16[2,1,16,8]{2,3,1,0:T(8,128)(2,1)S(1)}, bf16[2,1,16,8]{2,3,1,0:T(8,128)(2,1)}, u32[]{:S(2)}) copy-start(bf16[2,1,16,8]{2,3,1,0:T(8,128)(2,1)} %param.26) | copy-start | bytes 1540

commit v4 on v3

--- a/solution.py
+++ b/solution.py
@@ -147,10 +147,11 @@
 
 
 GROUP = H // KVH
-EXTRA = 128
-
-
-def attention_kernel(q_ref, k_ref, v_ref, xk_ref, xv_ref, mask_ref, xmask_ref, out_ref):
+
+
+def attention_kernel(
+    q_ref, k_ref, v_ref, nk_ref, nv_ref, mask_ref, xmask_ref, first_ref, drift_ref, out_ref
+):
     scale = HD ** (-0.5)
     keys, values = k_ref[...], v_ref[...]
     row_count = q_ref.shape[1]
@@ -161,7 +162,9 @@
         nt = (((1,), (1,)), ((), ()))
         scores = lax.dot_general(q, keys, nt, preferred_element_type=jnp.float32)
         scores = scores * scale + mask_ref[step]
-        extra = lax.dot_general(q, xk_ref[step], nt, preferred_element_type=jnp.float32)
+        extra_keys = jnp.concatenate([nk_ref[step], nk_ref[0]], axis=0)
+        extra_values = jnp.concatenate([nv_ref[step], nv_ref[0]], axis=0)
+        extra = lax.dot_general(q, extra_keys, nt, preferred_element_type=jnp.float32)
         extra = extra * scale + xmask_ref[step]
         peak = jnp.maximum(
             jnp.max(scores, axis=1, keepdims=True), jnp.max(extra, axis=1, keepdims=True)
@@ -171,14 +174,20 @@
         denom = jnp.sum(scores, axis=1, keepdims=True) + jnp.sum(extra, axis=1, keepdims=True)
         mixed = jnp.dot(scores.astype(jnp.bfloat16), values, preferred_element_type=jnp.float32)
         mixed += jnp.dot(
-            extra.astype(jnp.bfloat16), xv_ref[step], preferred_element_type=jnp.float32
+            extra.astype(jnp.bfloat16), extra_values, preferred_element_type=jnp.float32
         )
         mixed = mixed / denom
         for g in range(GROUP):
-            out_ref[step, :, g * HD : (g + 1) * HD] = mixed[g * row_count : (g + 1) * row_count]
-
-
-def attend_both(keys, values, length, drift, queries, new_keys, new_values):
+            columns = slice(g * HD, (g + 1) * HD)
+            block = mixed[g * row_count : g * row_count + BLOCK]
+            if step == 0:
+                block = block + first_ref[:, columns].astype(jnp.float32)
+            drifted = mixed[g * row_count + BLOCK : (g + 1) * row_count]
+            out_ref[step, :BLOCK, columns] = block
+            out_ref[step, BLOCK:, columns] = drifted + drift_ref[step, :, columns].astype(jnp.float32)
+
+
+def attend_both(keys, values, length, drift, queries, new_keys, new_values, first, drift_in):
     row_count, slots = queries.shape[1], keys.shape[0]
     places = jnp.arange(slots)
     hit = jnp.any(places[None, None, :] == drift[:, :, None], axis=1)
@@ -191,14 +200,9 @@
     fresh = jnp.ones((2, row_count, row_count - BLOCK), bool)
     older = jnp.stack([jnp.zeros_like(kept), kept])[:, None, :]
     older = jnp.broadcast_to(older, (2, row_count, kept.shape[0]))
-    rest = jnp.zeros((2, row_count, EXTRA - row_count - kept.shape[0]), bool)
-    xmask = jnp.where(jnp.concatenate([own, fresh, older, rest], axis=2), 0.0, -1e30)
+    none = jnp.zeros((2, row_count, BLOCK), bool)
+    xmask = jnp.where(jnp.concatenate([own, fresh, none, older], axis=2), 0.0, -1e30)
     xmask = jnp.tile(xmask.astype(jnp.float32), (1, GROUP, 1))
-
-    def extras(new):
-        again = jnp.broadcast_to(new[:1, BLOCK:], (2, row_count - BLOCK, new.shape[2]))
-        joined = jnp.concatenate([new, again], axis=1)
-        return jnp.pad(joined, ((0, 0), (0, EXTRA - joined.shape[1]), (0, 0)))
 
     wide = GROUP * HD
     return pl.pallas_call(
@@ -208,16 +212,18 @@
             pl.BlockSpec((2, row_count, wide), lambda j: (0, 0, j)),
             pl.BlockSpec((slots, HD), lambda j: (0, j)),
             pl.BlockSpec((slots, HD), lambda j: (0, j)),
-            pl.BlockSpec((2, EXTRA, HD), lambda j: (0, 0, j)),
-            pl.BlockSpec((2, EXTRA, HD), lambda j: (0, 0, j)),
+            pl.BlockSpec((2, row_count, HD), lambda j: (0, 0, j)),
+            pl.BlockSpec((2, row_count, HD), lambda j: (0, 0, j)),
             pl.BlockSpec((2, 1, slots), lambda j: (0, 0, 0)),
-            pl.BlockSpec((2, GROUP * row_count, EXTRA), lambda j: (0, 0, 0)),
+            pl.BlockSpec((2, GROUP * row_count, 2 * row_count), lambda j: (0, 0, 0)),
+            pl.BlockSpec((BLOCK, wide), lambda j: (0, j)),
+            pl.BlockSpec((2, row_count - BLOCK, wide), lambda j: (0, 0, j)),
         ],
         out_specs=pl.BlockSpec((2, row_count, wide), lambda j: (0, 0, j)),
         out_shape=jax.ShapeDtypeStruct((2, row_count, H * HD), jnp.float32),
         compiler_params=pltpu.CompilerParams(vmem_limit_bytes=60 * 2**20),
         name="attention",
-    )(queries, keys, values, extras(new_keys), extras(new_values), mask, xmask)
+    )(queries, keys, values, new_keys, new_values, mask, xmask, first, drift_in)
 
 
 SLOTS = 32
@@ -245,7 +251,7 @@
             x,
             c,
         )
-        for k in (1, 2, 3)
+        for k in (1, 2)
     ]
 
     loads = [
@@ -258,7 +264,7 @@
     barrier = pltpu.get_barrier_semaphore()
     for peer in (core, a_side, b_side, *z_side[1:]):
         pl.semaphore_signal(barrier, inc=1, device_id=peer, device_id_type=pl.DeviceIdType.MESH)
-    pl.semaphore_wait(barrier, 6)
+    pl.semaphore_wait(barrier, 5)
 
     def remote(src, dst, send, recv, peer):
         return pltpu.make_async_remote_copy(
@@ -278,7 +284,7 @@
         elif d & 2:
             src, peer = d - 2, a_side
         else:
-            src, peer = 0, z_side[d // 8 + d % 2]
+            src, peer = d - d % 2 if d > 16 else 0, z_side[1 if d % 2 else 2]
         return remote(rows.at[src], rows.at[d], ag_send.at[d], ag_recv.at[d], peer)
 
     def core_copy(j):
@@ -295,7 +301,7 @@
 
     def z_copy(k):
         src = part.at[k // 2 * 16 + k % 2]
-        return remote(src, from_z.at[k], rs_send.at[28 + k], rs_recv.at[28 + k], z_side[k])
+        return remote(src, from_z.at[k], rs_send.at[28 + k], rs_recv.at[28 + k], z_side[2 - k % 2])
 
     width = wd.shape[1]
     tile = 256
@@ -340,6 +346,8 @@
         rows[0, :, width:] = tables[step]
 
         def forward(d):
+            if d == 16:
+                gather_copy(17).start()
             if d & 6 == 0:
                 gather_copy(2 + d).start()
             if d & 4 == 0:
@@ -351,7 +359,7 @@
                 gather_copy(d).wait_recv()
                 forward(d)
 
-        for d in (1, 16, 17):
+        for d in (16, 1):
             gather_copy(d).start()
         forward(0)
         pass_on(2, 1, 4, 3, 5, 16, 6, 18, 7)
@@ -384,6 +392,9 @@
             if r < 2:
                 a_copy(z_half * 2 + r).wait_recv()
                 total = total + from_a[z_half * 2 + r].astype(jnp.float32)
+            if (z_half, r) == (1, 0):
+                z_copy(3).wait_recv()
+                total = total + from_z[3].astype(jnp.float32)
             return total
 
         def hand_on(z_half, *places):
@@ -413,7 +424,7 @@
         hand_on(1, 0)
         hand_on(0, 3, 2, 1)
         total = summed(0, 0)
-        for k in (1, 2, 3):
+        for k in (1, 2):
             z_copy(k).wait_recv()
             total = total + from_z[k].astype(jnp.float32)
         result = (residual[...] + total).astype(jnp.bfloat16)
@@ -436,7 +447,7 @@
     cache_keys, cache_values, lengths, drift_rows, block_in, drift_in, queries, new_keys,
     new_values, norm_gain, expert_ids, gate_weights, w_gate, w_up, w_down,
 ):
-    attended = attend_both(
+    base = attend_both(
         cache_keys[0],
         cache_values[0],
         lengths[0],
@@ -444,10 +455,10 @@
         queries[:, 0],
         new_keys[:, 0],
         new_values[:, 0],
+        block_in[0],
+        drift_in[:, 0],
     )
     row_count, width = queries.shape[2], queries.shape[3]
-    first = jnp.stack([block_in[0], jnp.zeros_like(block_in[0])])
-    base = attended + jnp.concatenate([first, drift_in[:, 0]], axis=1).astype(jnp.float32)
     member = expert_ids[:, 0, :, :, None] == jnp.arange(128)
     tables = jnp.sum(jnp.where(member, gate_weights[:, 0, :, :, None], 0), axis=2)
     tables = tables.astype(jnp.bfloat16)

time: 142 us -> 139 us (0.979)
  other arithmetic: 5.97 us -> 2.48 us
    add x1 -> x0, other arithmetic: 1.87 us -> none  [on_device_close(): attended + jnp.concatenate([first, drift_in[:, 0]], axis=1).astype(jnp.fl...]
    concatenate x1 -> x0, other arithmetic: 1.6 us -> none  [extras(): joined = jnp.concatenate([new, again], axis=1)]
    broadcast_in_dim x5 -> x1, local copies, waits for them, and re-layouts: 1.45 us -> 0.01 us  [attend_both(): none = jnp.zeros((2, row_count, BLOCK), bool)]
where the time goes in v4:
time: 139 us
  Pallas kernels  131 us (94%)
  local copies, waits for them, and re-layouts  4.81 us (3%)
  other arithmetic  2.48 us (2%)
    pallas_call x1, Pallas kernels, on_device_close(): pl.pallas_call(expert_kernel, out_shape=jax.ShapeDtypeStruct((2, row_coun...  123 us
    pallas_call x1, Pallas kernels, attend_both(): pl.pallas_call(attention_kernel, grid=(KVH,), in_specs=[pl.BlockSpec((2,...  7.64 us

profile of v4, /device:TPU:0, one launch (start us, length us, event | category | flops | bytes accessed | tf_op | source)
XLA Modules:
  0.0 138.8 jit_solution(5045022554007836868)
XLA Ops:
  0.7 0.1 pad.3.clone
  0.7 0.1 pad.2.clone
  0.8 0.7 slice_bitcast_fusion.1
  1.5 0.2 compare_reduce_fusion
  1.7 0.1 broadcast_in_dim.59
  1.8 0.1 add_select_fusion.1
  1.9 0.8 copy.20
  2.7 0.8 fusion
  3.5 0.6 add_select_fusion.mask_ref
  4.1 0.8 copy.19
  4.9 0.7 fusion.2.tables
  5.6 0.7 tile.4
  6.3 7.6 %attention.1.base = f32[2,16,4096]{2,1,0:T(8,128)} custom-call(bf16[2,16,4096]{2,1,0:T(8,128)(2,1)} %bitcast.37, bf16[2048,512]{1,0:T(8,128)(2,1)} %bitcast.33, bf16[2048,512]{1,0:T(8,128)(2,1)} %bitcast.34, bf16[2,16,512]{2,1,0:T(8,128)(2,1)} %bitcast.40, bf16[2,16,512]{2,1,0:T(8,128)(2,1)} %bitcast.41, f32[2,1,2048]{2,1,0:T(1,128)} %add_select_fusion.mask_ref, ...), custom_call_target="tpu_custom_call" | custom-call | tf_op jit(solution)/shard_map/attention/pallas_call | solution.py:208
  13.9 123.2 %experts.1 = bf16[2,16,4096]{2,1,0:T(8,128)(2,1)} custom-call(f32[2,16,4096]{2,1,0:T(8,128)} %attention.1.base, bf16[2,16,128]{2,1,0:T(8,128)(2,1)} %fusion.2.tables, f32[1,4096]{1,0:T(1,128)} %bitcast.42, bf16[4096,512]{1,0:T(8,128)(2,1)} %bitcast.30, bf16[4096,512]{1,0:T(8,128)(2,1)} %bitcast.31, bf16[512,4096]{1,0:T(8,128)(2,1)} %bitcast.32), custom_call_target="tpu_custom_call" | custom-call | tf_op jit(solution)/shard_map/experts/pallas_call | solution.py:469
  137.2 1.7 %copy.24 = bf16[2,1,16,4096]{3,2,1,0:T(8,128)(2,1)} copy(bf16[2,1,16,4096]{3,2,1,0:T(8,128)(2,1)} %bitcast.35) | data formatting | bytes 524288
  (7 shorter events, 0.1 us)

commit v5 on v4

--- a/solution.py
+++ b/solution.py
@@ -362,7 +362,7 @@
         for d in (16, 1):
             gather_copy(d).start()
         forward(0)
-        pass_on(2, 1, 4, 3, 5, 16, 6, 18, 7)
+        pass_on(2, 1, 16, 3, 18, 17, 4, 5, 19, 6, 7)
 
         @pl.when(step == 0)
         def _():
@@ -372,9 +372,11 @@
         for d in range(8, 16):
             gather_copy(d).wait_recv()
         up_tile(0, 0)
-        pass_on(17, 20)
+        pass_on(20, 22)
         up_tile(0, 1)
-        pass_on(19, 22, 21, 23)
+        pass_on(21, 23)
+        down(8)
+        down(0)
         for d in range(24, SLOTS):
             gather_copy(d).wait_recv()
         up_tile(16, 0)
@@ -413,12 +415,10 @@
             core_copy(8 + r).start()
         down(16)
         hand_on(1, 7, 5, 6, 4)
-        down(8)
         for r in order:
             core_copy(r).start()
+        hand_on(0, 7, 5)
         hand_on(1, 3)
-        down(0)
-        hand_on(0, 7, 5)
         hand_on(1, 2, 1)
         hand_on(0, 6, 4)
         hand_on(1, 0)

time: 139 us -> 138 us (level)
  Pallas kernels: 131 us -> 129 us
    pallas_call x1, Pallas kernels: 123 us -> 122 us  [on_device_close(): pl.pallas_call(expert_kernel, out_shape=jax.ShapeDtypeStruct((2, row_coun...]
where the time goes in v5:
time: 138 us; the launch traced here: 137 us
  Pallas kernels  129 us (93%)
  local copies, waits for them, and re-layouts  4.81 us (3%)
  other arithmetic  2.48 us (2%)
    pallas_call x1, Pallas kernels, on_device_close(): pl.pallas_call(expert_kernel, out_shape=jax.ShapeDtypeStruct((2, row_coun...  122 us
    pallas_call x1, Pallas kernels, attend_both(): pl.pallas_call(attention_kernel, grid=(KVH,), in_specs=[pl.BlockSpec((2,...  7.64 us

profile of v5, /device:TPU:0, one launch (start us, length us, event | category | flops | bytes accessed | tf_op | source)
XLA Modules:
  0.0 137.2 jit_solution(17398583458435254718)
XLA Ops:
  0.7 0.1 pad.3.clone
  0.7 0.1 pad.2.clone
  0.8 0.7 slice_bitcast_fusion.1
  1.5 0.2 compare_reduce_fusion
  1.7 0.1 broadcast_in_dim.59
  1.8 0.1 add_select_fusion.1
  1.9 0.8 copy.20
  2.7 0.8 fusion
  3.5 0.6 add_select_fusion.mask_ref
  4.1 0.8 copy.19
  4.9 0.7 fusion.2.tables
  5.6 0.7 tile.4
  6.3 7.6 %attention.1.base = f32[2,16,4096]{2,1,0:T(8,128)} custom-call(bf16[2,16,4096]{2,1,0:T(8,128)(2,1)} %bitcast.37, bf16[2048,512]{1,0:T(8,128)(2,1)} %bitcast.33, bf16[2048,512]{1,0:T(8,128)(2,1)} %bitcast.34, bf16[2,16,512]{2,1,0:T(8,128)(2,1)} %bitcast.40, bf16[2,16,512]{2,1,0:T(8,128)(2,1)} %bitcast.41, f32[2,1,2048]{2,1,0:T(1,128)} %add_select_fusion.mask_ref, ...), custom_call_target="tpu_custom_call" | custom-call | tf_op jit(solution)/shard_map/attention/pallas_call | solution.py:208
  13.9 121.6 %experts.1 = bf16[2,16,4096]{2,1,0:T(8,128)(2,1)} custom-call(f32[2,16,4096]{2,1,0:T(8,128)} %attention.1.base, bf16[2,16,128]{2,1,0:T(8,128)(2,1)} %fusion.2.tables, f32[1,4096]{1,0:T(1,128)} %bitcast.42, bf16[4096,512]{1,0:T(8,128)(2,1)} %bitcast.30, bf16[4096,512]{1,0:T(8,128)(2,1)} %bitcast.31, bf16[512,4096]{1,0:T(8,128)(2,1)} %bitcast.32), custom_call_target="tpu_custom_call" | custom-call | tf_op jit(solution)/shard_map/experts/pallas_call | solution.py:469
  135.6 1.7 %copy.24 = bf16[2,1,16,4096]{3,2,1,0:T(8,128)(2,1)} copy(bf16[2,1,16,4096]{3,2,1,0:T(8,128)(2,1)} %bitcast.35) | data formatting | bytes 524288
  (7 shorter events, 0.1 us)
